TPU v7x, 1024 devices: a whole 4x8x16 slice. The times are simulated.
1024 devices in a mesh: aux: 16 (over z), ao: 64 (over x, y, core).
Axes of the slice: x: 4, y: 8, z: 16, core: 2. Of those that a mesh axis runs over, the one named last changes fastest.
Arguments:
- b_source: bfloat16 [64, 8, 2048, 1024], P(None, None, ('aux', 'ao')), may hold values from -0.3984375 to 0.3984375
- g_occ: bfloat16 [64, 1024], P('ao'), may hold values from -0.81 to 2.02, as said below
- g_virt: bfloat16 [64, 1024], P('ao'), may hold values from -0.81 to 2.02, as said below
- atom_sizes: int32 [64], replicated, may hold values from 16 to 32, as said below
- pair_cols: int32 [64, 8], P('ao'), may hold values from 0 to 63
- live_slots: int32 [64], P('ao'), may hold values from 1 to 8, as said below
Outputs:
- chi_blocks: float32 [2, 2048, 128], P(None, ('aux', 'ao'))
Inputs may be any that keep to these rules, and one draw needn't show every extreme that they name: `live_slots`: every draw has a row atom with all 8 slots live. `atom_sizes`: each atom has either 32 or half of 32 basis functions; both occur in every draw. `g_occ`: each block is a diagonal of positive entries with off-diagonal entries. `g_virt`: each block is a diagonal of positive entries with off-diagonal entries.
All inputs are finite; a program needn't handle non-finite values.
Results may differ from a plain program's by a relative error of at most 0.00033.
Values may be sent and summed in bfloat16 or wider, within the bound.
A program may use at most 64 MiB of HBM per device.

v0:
```python
import jax
import jax.numpy as jnp
from jax import lax
from jax.sharding import PartitionSpec as P

NB = 32


def shifted(value, axis, steps):
    count = lax.axis_size(axis)
    pairs = [(source, (source + steps) % count) for source in range(count)]
    return lax.ppermute(value, axis, pairs)


def pad_masks(row_sizes, col_sizes, live_count, slot_count):
    lane_index = jnp.arange(NB)
    row_ok = lane_index[None, :] < row_sizes[:, None]
    col_ok = lane_index[None, None, :] < col_sizes[:, :, None]
    slot_ok = jnp.arange(slot_count)[None, :] < live_count[:, None]
    joined = row_ok[:, None, :, None] & col_ok[:, :, None, :] & slot_ok[:, :, None, None]
    return joined.reshape(row_sizes.shape[0], slot_count, NB * NB).astype(jnp.bfloat16)


def contract(masked, occ_tiles, virt_tiles):
    row_count, slot_count, aux_count, entries = masked.shape
    shaped = masked.reshape(row_count, slot_count, aux_count, NB, NB)
    half_done = jnp.einsum(
        "rml,rkpls->rkpms", occ_tiles, shaped, preferred_element_type=jnp.float32
    )
    half_done = half_done.astype(jnp.bfloat16)
    full_done = jnp.einsum(
        "rkpms,rksn->rkpmn", half_done, virt_tiles, preferred_element_type=jnp.float32
    )
    return full_done.reshape(row_count, slot_count, aux_count, entries).astype(jnp.bfloat16)


def local(b_source, g_occ, g_virt, atom_sizes, pair_cols, live_slots):
    remapped = lax.all_to_all(b_source, "ao", split_axis=0, concat_axis=2, tiled=True)
    row_count = g_occ.shape[0]
    slot_count = pair_cols.shape[1]
    first_row = lax.axis_index("ao") * row_count
    row_sizes = lax.dynamic_slice_in_dim(atom_sizes, first_row, row_count, 0)
    all_virt = lax.all_gather(g_virt, "ao", axis=0, tiled=True)
    pad_mask = pad_masks(row_sizes, atom_sizes[pair_cols], live_slots, slot_count)
    occ_tiles = g_occ.reshape(row_count, NB, NB)
    virt_tiles = all_virt[pair_cols].reshape(row_count, slot_count, NB, NB)
    masked = remapped * pad_mask[:, :, None, :]
    contracted = contract(masked, occ_tiles, virt_tiles)
    prior_terms = shifted(contracted, "aux", 1)
    same_block = jnp.einsum("rkpb,rkqb->pq", contracted, masked, preferred_element_type=jnp.float32)
    cross_block = jnp.einsum(
        "rkpb,rkqb->pq", prior_terms, masked, preferred_element_type=jnp.float32
    )
    return lax.psum_scatter(
        jnp.stack([same_block, cross_block]), "ao", scatter_dimension=1, tiled=True
    )


def solution(mesh):
    return jax.shard_map(
        local,
        mesh=mesh,
        in_specs=(
            P(None, None, ("aux", "ao"), None),
            P("ao", None),
            P("ao", None),
            P(),
            P("ao", None),
            P("ao"),
        ),
        out_specs=P(None, ("aux", "ao"), None),
        check_vma=False,
    )
```

profile of v0, /device:TPU:1, one launch (start us, length us, event | category | flops | bytes accessed | tf_op | source)
XLA Modules:
  0.0 412.6 jit_solution(2451787372172339916)
XLA Ops:
  6.5 3.5 copy.27
  10.1 18.4 %all-to-all-start = ((bf16[64,8,2,1024]{3,1,2,0:T(8,128)(2,1)}), bf16[64,8,2,1024]{3,1,2,0:T(8,128)(2,1)S(1)}, u32[]{:S(2)}, u32[]{:S(2)}) async-start(bf16[64,8,2,1024]{3,1,2,0:T(8,128)(2,1)} %copy.27), calls=%async_computation | async-start | bytes 4194304 | tf_op jit(solution)/shard_map/all_to_all | solution.py:38
  28.6 0.6 gather_fusion
  29.3 0.1 and.48
  30.1 0.6 dynamic_slice.3
  30.7 0.6 iota_compare_fusion.2
  31.6 77.8 %all-gather = bf16[64,1,1024]{2,1,0:T(2,128)(2,1)S(1)} all-gather(bf16[1,1,1024]{2,1,0:T(2,128)(2,1)S(1)} %bitcast.55), channel_id=1, replica_groups=mesh['aux'=16,'ao'=64] {'ao'}, dimensions={0}, use_global_device_ids=true | all-gather | bytes 133120 | tf_op jit(solution)/shard_map/all_gather | solution.py:43
  109.4 0.6 gather_fusion.1
  110.0 0.1 reshape.151
  110.2 1.5 bitcast_multiply_fusion.1
  111.7 10.9 %mul.23 = bf16[8,128,32,32]{3,2,0,1:T(8,128)(2,1)} reshape(bf16[1,8,64,2,1024]{4,1,3,2,0:T(8,128)(2,1)} %bitcast_multiply_fusion.1) | data formatting | bytes 4194304 | tf_op jit(solution)/shard_map/mul | solution.py:47
  122.6 13.2 %copy.28 = bf16[8,128,32,32]{1,2,3,0:T(8,128)(2,1)} copy(bf16[8,128,32,32]{3,2,0,1:T(8,128)(2,1)} %mul.23) | data formatting | bytes 4194304 | tf_op jit(solution)/shard_map/mul | solution.py:47
  135.8 2.3 convert_bitcast_fusion
  138.1 2.3 fusion.4
  140.4 3.9 copy.33
  144.3 2.2 collective-permute-start
  146.6 0.3 bitcast_multiply_fusion
  146.9 2.5 fusion.10
  149.4 52.4 %collective-permute-done = bf16[1,8,128,1024]{3,2,1,0:T(8,128)(2,1)S(1)} collective-permute-done((bf16[1,8,128,1024]{3,2,1,0:T(8,128)(2,1)}, bf16[1,8,128,1024]{3,2,1,0:T(8,128)(2,1)S(1)}, u32[]{:S(2)}, u32[]{:S(2)}) %collective-permute-start) | collective-permute-done | bytes 2097184 | tf_op jit(solution)/shard_map/ppermute | solution.py:12
  201.8 2.6 fusion.13
  204.4 0.7 pad_maximum_fusion
  205.1 1.3 dynamic-slice
  207.0 197.4 %all-reduce.3.cloned.1.call-done = f32[2,128,128]{2,1,0:T(8,128)} async-done(((f32[2,128,128]{2,1,0:T(8,128)}), f32[2,128,128]{2,1,0:T(8,128)}) %all-reduce.3.cloned.1.call-update) | async-done | bytes 131088
  404.4 1.3 constant_dynamic-slice_fusion
  (24 shorter events, 0.6 us)
Async XLA Ops:
  10.1 18.5 %copy-start.4 = (s32[1,8]{1,0:T(1,128)S(1)}, s32[1,8]{1,0:T(1,128)}, u32[]{:S(2)}) copy-start(s32[1,8]{1,0:T(1,128)} %param.10) | copy-start | bytes 100
  10.1 18.5 %copy-start = (s32[64]{0:T(128)S(1)}, s32[64]{0:T(128)}, u32[]{:S(2)}) copy-start(s32[64]{0:T(128)} %param.9) | copy-start | bytes 772
  10.1 21.4 %copy-start.3 = (bf16[1,1024]{1,0:T(2,128)(2,1)S(1)}, bf16[1,1024]{1,0:T(2,128)(2,1)}, u32[]{:S(2)}) copy-start(bf16[1,1024]{1,0:T(2,128)(2,1)} %param.7) | copy-start | bytes 6148
  10.1 21.5 %copy-start.2 = (bf16[1,1024]{1,0:T(2,128)(2,1)S(1)}, bf16[1,1024]{1,0:T(2,128)(2,1)}, u32[]{:S(2)}) copy-start(bf16[1,1024]{1,0:T(2,128)(2,1)} %param.8) | copy-start | bytes 6148
  10.1 100.1 %all-to-all-start = ((bf16[64,8,2,1024]{3,1,2,0:T(8,128)(2,1)}), bf16[64,8,2,1024]{3,1,2,0:T(8,128)(2,1)S(1)}, u32[]{:S(2)}, u32[]{:S(2)}) async-start(bf16[64,8,2,1024]{3,1,2,0:T(8,128)(2,1)} %copy.27), calls=%async_computation | async-start | bytes 4194304 | tf_op jit(solution)/shard_map/all_to_all | solution.py:38
  28.5 375.9 %all-reduce.3.cloned.1.call-start = ((), (), s32[]{:S(2)}) async-start(), calls=%async_computation.1 | async-start | bytes 262144
  144.3 2.5 copy-start.1
  144.3 57.5 %collective-permute-start = (bf16[1,8,128,1024]{3,2,1,0:T(8,128)(2,1)}, bf16[1,8,128,1024]{3,2,1,0:T(8,128)(2,1)S(1)}, u32[]{:S(2)}, u32[]{:S(2)}) collective-permute-start(bf16[1,8,128,1024]{3,2,1,0:T(8,128)(2,1)} %copy.33), channel_id=1, source_target_pairs={{0,64},{64,128},{128,192},{192,256},{256,320},{320,384},{384,448},... | collective-permute-start | bytes 6291464 | tf_op jit(solution)/shard_map/ppermute | solution.py:12
Sparse Core Ops, SparseCore 0:
  205.2 199.1 all-reduce.2
where the time goes:
time: 413 us
  waiting for transfers between devices  250 us (61%)
  blocking collectives  77.8 us (19%)
  local copies, waits for them, and re-layouts  36.5 us (9%)
  starting transfers between devices  20.7 us (5%)
  between operations  14.9 us (4%)
  matrix products  9.68 us (2%)
    unnamed x2, waiting for transfers between devices  197 us
    all_gather x1, blocking collectives, local(): all_virt = lax.all_gather(g_virt, 'ao', axis=0, tiled=True)  77.8 us
    ppermute x1, waiting for transfers between devices, shifted(): return lax.ppermute(value, axis, pairs)  52.4 us
    mul x2, local copies, waits for them, and re-layouts, local(): masked = remapped * pad_mask[:, :, None, :]  24.2 us
    all_to_all x1, starting transfers between devices, local(): lax.all_to_all(b_source, 'ao', split_axis=0, concat_axis=2, tiled=True)  18.4 us
  transfers between devices with their start and end apart: 3, of which 2 were waited for; matrix products, arithmetic and copies ran while one was open for 2% of the time, Pallas kernels for 0%

commit v1 on v0

v1 whole, which is shorter than its diff:
```python
import functools

import jax
import jax.numpy as jnp
from jax import lax
from jax.experimental import pallas as pl
from jax.experimental.pallas import tpu as pltpu
from jax.sharding import PartitionSpec as P

MESH = pl.DeviceIdType.MESH
F32 = jnp.float32
BF16 = jnp.bfloat16
NB = 32
TILE = NB * NB
QUART = 256
HALF = 128
SLOTS = 8
CORES = 2


def iota(shape, dim):
    return lax.broadcasted_iota(jnp.int32, shape, dim)


def dot(a, b):
    return lax.dot_general(a, b, (((1,), (0,)), ((), ())), preferred_element_type=F32)


def dot_nt(a, b):
    return lax.dot_general(a, b, (((1,), (1,)), ((), ())), preferred_element_type=F32)


def ones_where(cond):
    return jnp.where(cond, 1.0, 0.0).astype(BF16)


def pick(rows, cond):
    return jnp.sum(jnp.where(cond, rows, 0.0), axis=0, keepdims=True)


def lane_sum(values):
    return jnp.sum(values, axis=1, keepdims=True)


def wait_bytes(ref, sem):
    pltpu.make_async_copy(ref, ref, sem).wait()


def kernel(
    dims, b_hbm, meta_own, g_own, sizes, out_ref, flag_ref,
    b_in, bq, meta, table, send, recv, zup, zdown, masked, masked_up, masked_down, contr,
    w1, w2, v1, v2, same, cross, back_send, back_recv, rs_a, rs_a_in, rs_mid, rs_b, rs_b_in,
    b_sem, meta_sem, table_sem, small_send, send_sem, recv_sem, zs_sem, zu_sem, zd_sem, back_sem, rs_sem,
):
    span, up_span, n_x, n_y, n_z = dims
    n_grp = n_y * CORES
    n_ao = n_x * n_grp
    n_p = 2 * n_ao
    n_c = n_ao * SLOTS * 2
    me = lax.axis_index("ao")
    zz = lax.axis_index("aux")
    above = lax.rem(zz + 1, n_z)
    below = lax.rem(zz + n_z - 1, n_z)
    my_x = me // n_grp
    my_in = lax.rem(me, n_grp)

    load_b = pltpu.make_async_copy(b_hbm, b_in, b_sem)
    load_b.start()
    meta[pl.ds(me, 1)] = meta_own[...].reshape(1, 1, 128)
    table[pl.ds(me, 1)] = g_own[...].reshape(1, 16, 128)

    barrier = pltpu.get_barrier_semaphore()

    def greet(step, carry):
        peer = lax.rem(me + step, n_ao)
        pl.semaphore_signal(barrier, inc=1, device_id=(zz, peer), device_id_type=MESH)
        return carry

    lax.fori_loop(1, n_ao, greet, 0)
    pl.semaphore_signal(barrier, inc=1, device_id=(above, me), device_id_type=MESH)
    pl.semaphore_signal(barrier, inc=1, device_id=(below, me), device_id_type=MESH)
    pl.semaphore_wait(barrier, n_ao + 1)

    def tell_meta(step, carry):
        peer = lax.rem(me + step, n_ao)
        pltpu.make_async_remote_copy(
            src_ref=meta.at[me], dst_ref=meta.at[me], send_sem=small_send.at[0], recv_sem=meta_sem,
            device_id=(zz, peer), device_id_type=MESH,
        ).start()
        return carry

    lax.fori_loop(1, n_ao, tell_meta, 0)

    def tell_table(step, carry):
        peer = lax.rem(me + step, n_ao)
        pltpu.make_async_remote_copy(
            src_ref=table.at[me], dst_ref=table.at[me], send_sem=small_send.at[1], recv_sem=table_sem,
            device_id=(zz, peer), device_id_type=MESH,
        ).start()
        return carry

    lax.fori_loop(1, n_ao, tell_table, 0)

    lane_in, lane_out = iota((512, 512), 0), iota((512, 512), 1)
    moved = (lane_in // 16 % 2) * 256 + (lane_in // 32) * 16 + lane_in % 16
    mover = ones_where(moved == lane_out)
    load_b.wait()
    step_rows = n_c // 4

    def reorder(part, carry):
        rows = pl.ds(pl.multiple_of(part * step_rows, step_rows), step_rows)
        for mh in range(2):
            lanes = slice(mh * 512, (mh + 1) * 512)
            bq[rows, lanes] = dot(b_in[rows, lanes], mover).astype(BF16)
        return carry

    lax.fori_loop(0, 4, reorder, 0)

    c_row = iota((1, n_c), 1)
    c_atom, c_slot, c_aux = c_row // 16, c_row // 2 % 8, c_row % 2
    earlier = ones_where(
        (iota((n_c, n_c), 0) // 2 < iota((n_c, n_c), 1) // 2) & (iota((n_c, n_c), 0) % 2 == 0)
    )
    atom_col = iota((n_ao, n_c), 0)
    own_col = atom_col == iota((n_ao, n_c), 1) // 16
    slot_pick = ones_where(iota((128, n_c), 0) == iota((128, n_c), 1) // 2 % 8)
    size_col = sizes[...]
    row_big = pick(jnp.broadcast_to(size_col, (n_ao, n_c)), own_col) > 16.5

    wait_bytes(meta.at[pl.ds(0, n_ao - 1)], meta_sem)
    facts = meta[...].reshape(n_ao, 128)
    c_col = pick(dot(facts.astype(BF16), slot_pick), own_col)
    c_live = pick(jnp.broadcast_to(facts[:, 8:9], (n_ao, n_c)), own_col)
    col_big = pick(jnp.broadcast_to(size_col, (n_ao, n_c)), atom_col.astype(F32) == c_col) > 16.5
    alive = c_slot.astype(F32) < c_live
    one = jnp.ones((1, n_c), F32)
    nil = jnp.zeros((1, n_c), F32)
    big = jnp.where(row_big, one, nil)
    wide = jnp.where(col_big, one, nil)
    here = jnp.where(alive, one, nil)
    is4 = here * big * wide
    is2r = here * big * (one - wide)
    is2c = here * (one - big) * wide
    is2 = is2r + is2c
    is1 = here * (one - big) * (one - wide)
    marks = jnp.concatenate([is4, is2, is1, jnp.zeros((13, n_c), F32)], axis=0)
    before = dot(marks.astype(BF16), earlier)
    n4, n2, n1 = (lane_sum(value) * 0.5 for value in (is4, is2, is1))
    first = is4 * 4.0 * before[0:1] + is2 * (4.0 * n4 + 2.0 * before[1:2])
    first = first + is1 * (4.0 * n4 + 2.0 * n2 + before[2:3])
    c_auxf = c_aux.astype(F32)

    def numbered(member, offset):
        return jnp.where(member > 0.5, 2.0 * (first + offset) + c_auxf, -5.0)

    units = [
        numbered(here, 0.0),
        numbered(is4 + is2c, 1.0),
        numbered(is4 + is2r, is4 * 2.0 + is2r),
        numbered(is4, 3.0),
    ]
    total = 4.0 * n4 + 2.0 * n2 + n1
    flag_ref[...] = jnp.broadcast_to(jnp.where(total > 4.0 * span * n_ao, 1.0, 0.0), (8, 128))

    out_row = iota((n_grp * 8, 1), 0)
    out_row = (out_row // 8) * span * 8 + (out_row % 4) * 2 + out_row // 4 % 2

    def pack(turn, carry):
        grp = lax.rem(my_x + turn, n_x)
        base = grp * (n_grp * span * 8)
        for j in range(span):
            wanted = (out_row + (base + j * 8)).astype(F32)
            got = jnp.zeros((n_grp * 8, QUART), F32)
            for q in range(4):
                got = got + dot(ones_where(units[q] == wanted), bq[:, q * QUART:(q + 1) * QUART])
            both = [got[:, h * HALF:(h + 1) * HALF].reshape(n_grp, 8, HALF) for h in range(2)]
            send[pl.ds(grp * n_grp, n_grp), :, j * HALF:(j + 1) * HALF] = jnp.concatenate(both, axis=1).astype(BF16)

        def ship(step, inner):
            peer = grp * n_grp + lax.rem(my_in + step, n_grp)

            @pl.when(peer != me)
            def _():
                pltpu.make_async_remote_copy(
                    src_ref=send.at[peer], dst_ref=recv.at[me], send_sem=send_sem, recv_sem=recv_sem.at[turn],
                    device_id=(zz, peer), device_id_type=MESH,
                ).start()

            @pl.when(peer == me)
            def _():
                pltpu.make_async_copy(send.at[peer], recv.at[me], recv_sem.at[turn]).start()

            return inner

        lax.fori_loop(0, n_grp, ship, 0)
        return carry

    lax.fori_loop(0, n_x, pack, 0)

    pair = iota((span * 16, 1), 0)
    slot_base = (me * span + pair // 16) * 4
    lead = ((slot_base + pair // 4 % 4) * 2).astype(F32)
    tail = ((slot_base + pair % 4) * 2).astype(F32)
    c_tile = (c_row // 2).astype(F32)

    def describe(unit):
        tile, atom, col, quarter, valid = (jnp.zeros((span * 16, 1), F32) for _ in range(5))
        for q in range(4):
            hit = units[q] == unit
            tile = tile + lane_sum(jnp.where(hit, c_tile, 0.0))
            atom = atom + lane_sum(jnp.where(hit, c_atom.astype(F32), 0.0))
            col = col + lane_sum(jnp.where(hit, c_col, 0.0))
            count = lane_sum(jnp.where(hit, 1.0, 0.0))
            quarter = quarter + q * count
            valid = valid + count
        row_half = jnp.where(quarter > 1.5, 1.0, 0.0)
        return tile, atom, col, row_half, quarter - 2.0 * row_half, valid

    tile_a, atom_a, col_a, mh_a, nh_a, valid_a = describe(lead)
    tile_b, _, _, mh_b, nh_b, valid_b = describe(tail)
    joined = (tile_a == tile_b) & (valid_a > 0.5) & (valid_b > 0.5)
    index1 = jnp.where(joined & (nh_a == nh_b), atom_a * 16.0 + 4.0 * mh_b + 2.0 * mh_a, -9.0)
    index2 = jnp.where(joined & (mh_a == mh_b), col_a * 16.0 + 8.0 + 4.0 * nh_a + 2.0 * nh_b, -9.0)
    wait_bytes(table.at[pl.ds(0, n_ao - 1)], table_sem)
    greens = table[...].reshape(n_ao * 16, 128)
    g_lane = iota((span * 16, n_ao * 16), 1).astype(F32)
    for h in range(2):
        v1[:, h * HALF:(h + 1) * HALF] = dot(ones_where(g_lane == index1 + h), greens)
        v2[:, h * HALF:(h + 1) * HALF] = dot(ones_where(g_lane == index2 + h), greens)

    r, s = iota((QUART, QUART), 0), iota((QUART, QUART), 1)
    hi, lo = r // 16, r % 16
    spread1, gather1, keep1 = ones_where(hi == s % 16), ones_where(hi == s // 16), ones_where(lo == s % 16)
    spread2, gather2, keep2 = ones_where(lo == s // 16), ones_where(lo == s % 16), ones_where(hi == s // 16)

    def weights(j, carry):
        for a in range(4):
            for b in range(4):
                rows, lanes = slice(a * QUART, (a + 1) * QUART), slice(b * QUART, (b + 1) * QUART)
                if a + b == 3:
                    w1[j, rows, lanes] = jnp.zeros((QUART, QUART), BF16)
                    continue
                vec = v1[pl.ds(j * 16 + a * 4 + b, 1), :].astype(BF16)
                w1[j, rows, lanes] = dot(spread1 * vec, gather1).astype(BF16) * keep1
        for m in range(2):
            for a in range(2):
                for b in range(2):
                    vec = v2[pl.ds(j * 16 + (2 * m + a) * 4 + 2 * m + b, 1), :].astype(BF16)
                    w2[j, m, a * QUART:(a + 1) * QUART, b * QUART:(b + 1) * QUART] = (
                        dot(spread2 * vec, gather2).astype(BF16) * keep2
                    )
        return carry

    lax.fori_loop(0, span, weights, 0)

    o, i = iota((n_grp * 16, n_grp * 16), 0), iota((n_grp * 16, n_grp * 16), 1)
    went = (i // 8 % 2 * 4 + i % 4) * (2 * n_grp) + (i // 16) * 2 + i // 4 % 2
    sorter = ones_where(o == went)

    def unpack(source, grp, target, count):
        block = source[pl.ds(grp * n_grp, n_grp)].reshape(n_grp * 16, count * HALF)
        placed = dot(sorter, block).astype(BF16)
        rows = pl.ds(pl.multiple_of(grp * (2 * n_grp), 2 * n_grp), 2 * n_grp)
        for h in range(2):
            for b in range(4):
                part = placed[(h * 4 + b) * 2 * n_grp:(h * 4 + b + 1) * 2 * n_grp]
                for j in range(count):
                    target[j, rows, b * QUART + h * HALF:b * QUART + (h + 1) * HALF] = part[:, j * HALF:(j + 1) * HALF]

    down_span = span - up_span

    def arrive(turn, carry):
        grp = lax.rem(my_x + n_x - turn, n_x)
        block = pl.ds(grp * n_grp, n_grp)
        wait_bytes(recv.at[block], recv_sem.at[turn])
        pltpu.make_async_remote_copy(
            src_ref=recv.at[block, :, pl.ds(0, up_span * HALF)], dst_ref=zup.at[block],
            send_sem=zs_sem.at[0], recv_sem=zu_sem.at[turn], device_id=(above, me), device_id_type=MESH,
        ).start()
        pltpu.make_async_remote_copy(
            src_ref=recv.at[block, :, pl.ds(up_span * HALF, down_span * HALF)], dst_ref=zdown.at[block],
            send_sem=zs_sem.at[1], recv_sem=zd_sem.at[turn], device_id=(below, me), device_id_type=MESH,
        ).start()
        unpack(recv, grp, masked, span)
        return carry

    lax.fori_loop(0, n_x, arrive, 0)

    def contract(tiles, j):
        half = dot(tiles, w1[j]).astype(BF16)
        done = [dot(half[:, m * 512:(m + 1) * 512], w2[j, m]).astype(BF16) for m in range(2)]
        return jnp.concatenate(done, axis=1)

    same[...] = jnp.zeros_like(same)
    cross[...] = jnp.zeros_like(cross)
    back_send[...] = jnp.zeros_like(back_send)

    def own_slot(j, carry):
        tiles = masked[j]
        result = contract(tiles, j)
        contr[j] = result
        same[...] += dot_nt(result, tiles)
        return carry

    lax.fori_loop(0, span, own_slot, 0)

    def arrive_down(turn, carry):
        grp = lax.rem(my_x + n_x - turn, n_x)
        wait_bytes(zdown.at[pl.ds(grp * n_grp, n_grp)], zd_sem.at[turn])
        unpack(zdown, grp, masked_down, down_span)
        return carry

    lax.fori_loop(0, n_x, arrive_down, 0)

    def down_slot(j, carry):
        back_send[...] += dot_nt(contr[up_span + j], masked_down[j])
        return carry

    lax.fori_loop(0, down_span, down_slot, 0)
    back = pltpu.make_async_remote_copy(
        src_ref=back_send, dst_ref=back_recv, send_sem=back_sem.at[0], recv_sem=back_sem.at[1],
        device_id=(above, me), device_id_type=MESH,
    )
    back.start()

    def arrive_up(turn, carry):
        grp = lax.rem(my_x + n_x - turn, n_x)
        wait_bytes(zup.at[pl.ds(grp * n_grp, n_grp)], zu_sem.at[turn])
        unpack(zup, grp, masked_up, up_span)
        return carry

    lax.fori_loop(0, n_x, arrive_up, 0)

    def up_slot(j, carry):
        cross[...] += dot_nt(contract(masked_up[j], j), masked[j])
        return carry

    lax.fori_loop(0, up_span, up_slot, 0)
    back.wait()
    cross[...] += back_recv[...]

    my_y = my_in // CORES
    my_core = lax.rem(me, CORES)
    n_a = n_x * CORES
    mine = my_x * CORES + my_core
    for a in range(n_a):
        for c, part in enumerate((same, cross)):
            for e in range(2):
                start = (a // CORES) * n_grp * 2 + (a % CORES) * 2 + e
                rs_a[a, (c * 2 + e) * n_y:(c * 2 + e + 1) * n_y, :] = part[pl.ds(start, n_y, stride=4), :]
    rs_a_in[pl.ds(mine, 1)] = rs_a[pl.ds(mine, 1)]

    def copy_a(step):
        to = lax.rem(mine + step, n_a)
        peer = ((to // CORES) * n_y + my_y) * CORES + lax.rem(to, CORES)
        return pltpu.make_async_remote_copy(
            src_ref=rs_a.at[to], dst_ref=rs_a_in.at[mine], send_sem=rs_sem.at[0], recv_sem=rs_sem.at[1],
            device_id=(zz, peer), device_id_type=MESH,
        )

    for step in range(1, n_a):
        copy_a(step).start()
    wait_bytes(rs_a_in.at[pl.ds(0, n_a - 1)], rs_sem.at[1])
    rs_mid[...] = jnp.sum(rs_a_in[...], axis=0)
    for y in range(n_y):
        rs_b[y, 0:4, :] = rs_mid[pl.ds(y, 4, stride=n_y), :]
        rs_b[y, 4:8, :] = jnp.zeros((4, n_p), F32)
    rs_b_in[pl.ds(my_y, 1)] = rs_b[pl.ds(my_y, 1)]

    def copy_b(step):
        to = lax.rem(my_y + step, n_y)
        peer = (my_x * n_y + to) * CORES + my_core
        return pltpu.make_async_remote_copy(
            src_ref=rs_b.at[to], dst_ref=rs_b_in.at[my_y], send_sem=rs_sem.at[2], recv_sem=rs_sem.at[3],
            device_id=(zz, peer), device_id_type=MESH,
        )

    for step in range(1, n_y):
        copy_b(step).start()
    wait_bytes(rs_b_in.at[pl.ds(0, n_y - 1)], rs_sem.at[3])
    final = jnp.sum(rs_b_in[...], axis=0)
    out_ref[0] = final[0:2]
    out_ref[1] = final[2:4]

    wait_bytes(meta.at[pl.ds(0, n_ao - 1)], small_send.at[0])
    wait_bytes(table.at[pl.ds(0, n_ao - 1)], small_send.at[1])
    wait_bytes(send.at[pl.ds(0, n_ao - 1)], send_sem)
    wait_bytes(zup, zs_sem.at[0])
    wait_bytes(zdown, zs_sem.at[1])
    wait_bytes(rs_a.at[pl.ds(0, n_a - 1)], rs_sem.at[0])
    wait_bytes(rs_b.at[pl.ds(0, n_y - 1)], rs_sem.at[2])


def run(span, shape, ident, b_rows, meta_row, greens, sizes):
    n_x, n_y, n_z = shape
    n_ao = n_x * n_y * CORES
    n_c, n_p = n_ao * SLOTS * 2, 2 * n_ao
    up_span = span // 2
    down_span = span - up_span
    vmem = pl.BlockSpec(memory_space=pltpu.VMEM)
    dma = pltpu.SemaphoreType.DMA
    return pl.pallas_call(
        functools.partial(kernel, (span, up_span, n_x, n_y, n_z)),
        out_shape=(jax.ShapeDtypeStruct((2, 2, n_p), F32), jax.ShapeDtypeStruct((8, 128), F32)),
        in_specs=[pl.BlockSpec(memory_space=pl.ANY), vmem, vmem, vmem],
        out_specs=(vmem, vmem),
        scratch_shapes=[
            pltpu.VMEM((n_c, TILE), BF16),
            pltpu.VMEM((n_c, TILE), BF16),
            pltpu.VMEM((n_ao, 1, 128), F32),
            pltpu.VMEM((n_ao, 16, 128), BF16),
            pltpu.VMEM((n_ao, 16, span * HALF), BF16),
            pltpu.VMEM((n_ao, 16, span * HALF), BF16),
            pltpu.VMEM((n_ao, 16, up_span * HALF), BF16),
            pltpu.VMEM((n_ao, 16, down_span * HALF), BF16),
            pltpu.VMEM((span, n_p, TILE), BF16),
            pltpu.VMEM((up_span, n_p, TILE), BF16),
            pltpu.VMEM((down_span, n_p, TILE), BF16),
            pltpu.VMEM((span, n_p, TILE), BF16),
            pltpu.VMEM((span, TILE, TILE), BF16),
            pltpu.VMEM((span, 2, 512, 512), BF16),
            pltpu.VMEM((span * 16, QUART), F32),
            pltpu.VMEM((span * 16, QUART), F32),
            pltpu.VMEM((n_p, n_p), F32),
            pltpu.VMEM((n_p, n_p), F32),
            pltpu.VMEM((n_p, n_p), F32),
            pltpu.VMEM((n_p, n_p), F32),
            pltpu.VMEM((n_x * CORES, 4 * n_y, n_p), F32),
            pltpu.VMEM((n_x * CORES, 4 * n_y, n_p), F32),
            pltpu.VMEM((4 * n_y, n_p), F32),
            pltpu.VMEM((n_y, 8, n_p), F32),
            pltpu.VMEM((n_y, 8, n_p), F32),
            dma, dma, dma, dma((2,)), dma, dma((n_x,)), dma((2,)), dma((n_x,)), dma((n_x,)), dma((2,)), dma((4,)),
        ],
        compiler_params=pltpu.CompilerParams(
            collective_id=ident, has_side_effects=True, vmem_limit_bytes=56 * 1024 * 1024
        ),
        name=f"blocks_{span}",
    )(b_rows, meta_row, greens, sizes)


def quarters(blocks):
    return blocks.reshape(2, 16, 2, 16).transpose(0, 2, 1, 3).reshape(8, 128)


def local(shape, b_source, g_occ, g_virt, atom_sizes, pair_cols, live_slots):
    n_ao = atom_sizes.shape[0]
    b_rows = b_source.reshape(n_ao * SLOTS * 2, TILE)
    meta_row = jnp.concatenate([pair_cols, live_slots[:, None], jnp.zeros((1, 119), jnp.int32)], axis=1).astype(F32)
    greens = jnp.concatenate([quarters(g_occ), quarters(g_virt)], axis=0)
    sizes = atom_sizes.astype(F32)[:, None]
    short, flag = run(4, shape, 0, b_rows, meta_row, greens, sizes)

    def whole(values):
        return run(8, shape, 1, *values)[0]

    return lax.cond(flag[0, 0] > 0.5, whole, lambda values: short, (b_rows, meta_row, greens, sizes))


def solution(mesh):
    n_ao, n_z = mesh.shape["ao"], mesh.shape["aux"]
    n_x = 4 if n_ao >= 64 else 2
    return jax.shard_map(
        functools.partial(local, (n_x, n_ao // (n_x * CORES), n_z)),
        mesh=mesh,
        in_specs=(
            P(None, None, ("aux", "ao"), None),
            P("ao", None),
            P("ao", None),
            P(),
            P("ao", None),
            P("ao"),
        ),
        out_specs=P(None, ("aux", "ao"), None),
        check_vma=False,
    )
```

time: 413 us -> 86.7 us (0.21)
  waiting for transfers between devices: 250 us -> 0 us
  blocking collectives: 77.8 us -> 0 us
  Pallas kernels: 0 us -> 76.3 us
  local copies, waits for them, and re-layouts: 36.5 us -> 5.59 us
  starting transfers between devices: 20.7 us -> 0 us
  between operations: 14.9 us -> 1.35 us
  matrix products: 9.68 us -> 0 us
    unnamed x2 -> x0, waiting for transfers between devices: 197 us -> none
    all_gather x1 -> x0, blocking collectives: 77.8 us -> none  [local(): all_virt = lax.all_gather(g_virt, 'ao', axis=0, tiled=True)]
    pallas_call x0 -> x1, Pallas kernels: none -> 76.3 us  [run(): pl.pallas_call(functools.partial(kernel, (span, up_span, n_x, n_y, n_z)),...]
    ppermute x1 -> x0, waiting for transfers between devices: 52.4 us -> none  [shifted(): return lax.ppermute(value, axis, pairs)]
    mul x2 -> x0, local copies, waits for them, and re-layouts: 24.2 us -> none  [local(): masked = remapped * pad_mask[:, :, None, :]]
    all_to_all x1 -> x0, starting transfers between devices: 18.4 us -> none  [local(): lax.all_to_all(b_source, 'ao', split_axis=0, concat_axis=2, tiled=True)]
    dot_general x4 -> x0, matrix products: 9.68 us -> none  [the longest x1 2.57 us: local(): jnp.einsum('rkpb,rkqb->pq', prior_terms, masked, preferred_element_type=j...]
    unnamed x14 -> x2, local copies, waits for them, and re-layouts: 6.15 us -> 0.59 us
  transfers between devices with their start and end apart: 3 -> 0, of which waited for: 2 -> 0; matrix products, arithmetic and copies ran while one was open for 2% -> 0% of each run, Pallas kernels for 0% -> 0%
where the time goes in v1:
time: 86.7 us; the launch traced here: 86.3 us
  Pallas kernels  76.3 us (88%)
  local copies, waits for them, and re-layouts  5.59 us (6%)
  other arithmetic  2.81 us (3%)
  between operations  1.35 us (2%)
    pallas_call x1, Pallas kernels, run(): pl.pallas_call(functools.partial(kernel, (span, up_span, n_x, n_y, n_z)),...  76.3 us
    reshape x1, local copies, waits for them, and re-layouts, local(): b_rows = b_source.reshape(n_ao * SLOTS * 2, TILE)  2.75 us

profile of v1, /device:TPU:1, one launch (start us, length us, event | category | flops | bytes accessed | tf_op | source)
XLA Modules:
  0.0 86.3 jit_solution(295219925047353144)
XLA Ops:
  0.7 0.7 convert_bitcast_fusion
  1.3 0.7 fusion.meta_own
  2.0 0.7 reduce
  2.8 0.7 reduce.1
  3.5 0.1 reshape.62
  3.6 0.1 reshape.63
  3.6 0.1 reshape.60
  3.7 0.1 reshape.61
  3.8 0.7 copy.11.sizes
  4.6 2.7 %reshape.59.b_hbm = bf16[1024,1024]{1,0:T(8,128)(2,1)S(1)} reshape(bf16[64,8,2,1024]{3,2,1,0:T(2,128)(2,1)} %param.8) | data formatting | bytes 4194304 | tf_op jit(solution)/shard_map/reshape | solution.py:448
  7.3 76.3 %blocks_4.1 = (f32[2,2,128]{2,1,0:T(2,128)S(1)}, f32[8,128]{1,0:T(8,128)}) custom-call(bf16[1024,1024]{1,0:T(8,128)(2,1)S(1)} %reshape.59.b_hbm, f32[1,128]{1,0:T(1,128)S(1)} %fusion.meta_own, bf16[16,128]{1,0:T(8,128)(2,1)S(1)} %constant_dynamic-update-slice_fusion.g_own, f32[64,1]{1,0:T(8,128)} %copy.11.sizes), custom_call_target="tpu_custom_call" | custom-call | tf_op jit(solution)/shard_map/blocks_4/pallas_call | solution.py:402
  83.7 1.2 %slice.3 = f32[1,1]{1,0:T(1,128)} slice(f32[8,128]{1,0:T(8,128)} %get-tuple-element.24), slice={[0:1], [0:1]} | slice | bytes 8 | tf_op jit(solution)/shard_map/slice | solution.py:457
  85.5 0.2 conditional.1
  85.7 0.6 copy.22
  (5 shorter events, 0.0 us)

commit v2 on v0

v2 whole, which is shorter than its diff:
```python
import functools

import jax
import jax.numpy as jnp
from jax import lax
from jax.experimental import pallas as pl
from jax.experimental.pallas import tpu as pltpu
from jax.sharding import PartitionSpec as P

MESH = pl.DeviceIdType.MESH
F32 = jnp.float32
BF16 = jnp.bfloat16
NB = 32
TILE = NB * NB
QUART = 256
HALF = 128
SLOTS = 8
CORES = 2


def iota(shape, dim):
    return lax.broadcasted_iota(jnp.int32, shape, dim)


def dot(a, b):
    return lax.dot_general(a, b, (((1,), (0,)), ((), ())), preferred_element_type=F32)


def dot_nt(a, b):
    return lax.dot_general(a, b, (((1,), (1,)), ((), ())), preferred_element_type=F32)


def ones_where(cond):
    return jnp.where(cond, 1.0, 0.0).astype(BF16)


def pick(rows, cond):
    return jnp.sum(jnp.where(cond, rows, 0.0), axis=0, keepdims=True)


def lane_sum(values):
    return jnp.sum(values, axis=1, keepdims=True)


def wait_bytes(ref, sem):
    pltpu.make_async_copy(ref, ref, sem).wait()


def kernel(
    dims, b_hbm, pairs_own, live_own, occ_own, virt_own, sizes, out_ref, flag_ref,
    b_in, bq, meta, table, send, recv, zup, masked, masked_up, w1, w2, v1, v2,
    same, cross, rs_a, rs_a_in, rs_mid, rs_b, rs_b_in,
    b_sem, meta_sem, table_sem, small_send, send_sem, recv_sem, zs_sem, zu_sem, rs_sem,
):
    caps, n_x, n_y, n_z = dims
    span = max(caps)
    n_grp = n_y * CORES
    n_ao = n_x * n_grp
    n_p = 2 * n_ao
    n_c = n_ao * SLOTS * 2
    me = lax.axis_index("ao")
    zz = lax.axis_index("aux")
    above = lax.rem(zz + 1, n_z)
    below = lax.rem(zz + n_z - 1, n_z)
    my_x = me // n_grp
    my_in = lax.rem(me, n_grp)
    my_y = my_in // CORES
    my_core = lax.rem(me, CORES)

    def device(x, y, core):
        return (x * n_y + y) * CORES + core

    def by_core(core, act):
        if caps[0] == caps[1]:
            act(0, caps[0])
            return
        for c in range(CORES):
            pl.when(core == c)(functools.partial(act, c, caps[c]))

    load_b = pltpu.make_async_copy(b_hbm, b_in, b_sem)
    load_b.start()
    if min(caps) < span:
        unused = slice(min(caps) * HALF, span * HALF)
        for buffer in (recv, zup):
            buffer[:, :, unused] = jnp.zeros((n_ao, 16, (span - min(caps)) * HALF), BF16)

    spot = (my_core * n_x + my_x) * n_y + my_y
    line = (my_core * n_x + my_x) * n_y
    lane = iota((1, 128), 1)
    facts = jnp.where(lane == SLOTS, live_own[...].astype(F32), jnp.zeros((1, 128), F32))
    pairs = pairs_own[...].astype(F32)
    for k in range(SLOTS):
        facts = jnp.where(lane == k, pairs[:, k:k + 1], facts)
    meta[pl.ds(spot, 1)] = facts.reshape(1, 1, 128)
    greens = [own[:, i * 128:(i + 1) * 128].astype(F32) for own in (occ_own[...], virt_own[...]) for i in range(8)]
    table[pl.ds(spot, 1)] = jnp.concatenate(greens, axis=0).astype(BF16).reshape(1, 16, 128)

    barrier = pltpu.get_barrier_semaphore()

    def greet(step, carry):
        peer = lax.rem(me + step, n_ao)
        pl.semaphore_signal(barrier, inc=1, device_id=(zz, peer), device_id_type=MESH)
        return carry

    pl.semaphore_signal(barrier, inc=1, device_id=(below, me), device_id_type=MESH)
    lax.fori_loop(1, n_ao, greet, 0)

    lane_in, lane_out = iota((512, 512), 0), iota((512, 512), 1)
    moved = (lane_in // 16 % 2) * 256 + (lane_in // 32) * 16 + lane_in % 16
    mover = ones_where(moved == lane_out)
    part_atoms = n_ao // 4
    part_rows = part_atoms * SLOTS * 2

    def reorder(part, carry):
        loaded = b_in[pl.ds(part * part_atoms, part_atoms)].reshape(part_rows, TILE)
        rows = pl.ds(pl.multiple_of(part * part_rows, part_rows), part_rows)
        for mh in range(2):
            placed = dot(loaded[:, mh * 512:(mh + 1) * 512], mover).astype(BF16)
            bq[2 * mh, rows, :] = placed[:, :QUART]
            bq[2 * mh + 1, rows, :] = placed[:, QUART:]
        return carry

    pl.semaphore_wait(barrier, n_ao)

    def spread_y(ref, send_to, recv_from):
        def one(step, carry):
            peer = device(my_x, lax.rem(my_y + step, n_y), my_core)
            pltpu.make_async_remote_copy(
                src_ref=ref.at[spot], dst_ref=ref.at[spot], send_sem=send_to, recv_sem=recv_from,
                device_id=(zz, peer), device_id_type=MESH,
            ).start()
            return carry

        lax.fori_loop(1, n_y, one, 0)

    n_a = n_x * CORES
    mine = my_x * CORES + my_core

    def spread_x(ref, send_to, recv_from):
        block = pl.ds(line, n_y)

        def one(step, carry):
            to = lax.rem(mine + step, n_a)
            pltpu.make_async_remote_copy(
                src_ref=ref.at[block], dst_ref=ref.at[block], send_sem=send_to, recv_sem=recv_from,
                device_id=(zz, device(to // CORES, my_y, lax.rem(to, CORES))), device_id_type=MESH,
            ).start()
            return carry

        lax.fori_loop(1, n_a, one, 0)

    n_far = (n_a - 1) * n_y
    spread_y(meta, small_send.at[0], meta_sem.at[0])
    load_b.wait()
    lax.fori_loop(0, 2, reorder, 0)
    wait_bytes(meta.at[pl.ds(0, n_y - 1)], meta_sem.at[0])
    spread_x(meta, small_send.at[2], meta_sem.at[1])
    spread_y(table, small_send.at[1], table_sem.at[0])
    lax.fori_loop(2, 4, reorder, 0)

    c_row = iota((1, n_c), 1)
    c_atom, c_slot, c_aux = c_row // 16, c_row // 2 % 8, c_row % 2
    earlier = ones_where((iota((128, 128), 0) // 2 < iota((128, 128), 1) // 2) & (iota((128, 128), 0) % 2 == 0))
    atom_col = iota((n_ao, n_c), 0)
    spot_col = device(atom_col // n_y % n_x, atom_col % n_y, atom_col // (n_x * n_y))
    own_col = spot_col == iota((n_ao, n_c), 1) // 16
    slot_pick = ones_where(iota((128, n_c), 0) == iota((128, n_c), 1) // 2 % 8)
    size_row = jnp.broadcast_to(sizes[...].astype(F32), (n_ao, n_ao))
    size_col = lane_sum(jnp.where(iota((n_ao, n_ao), 0) == iota((n_ao, n_ao), 1), size_row, 0.0))
    size_all = jnp.broadcast_to(size_col, (n_ao, n_c))
    row_big = pick(size_all, atom_col == iota((n_ao, n_c), 1) // 16) > 16.5

    wait_bytes(table.at[pl.ds(0, n_y - 1)], table_sem.at[0])
    spread_x(table, small_send.at[3], table_sem.at[1])
    wait_bytes(meta.at[pl.ds(0, n_far)], meta_sem.at[1])
    facts = meta[...].reshape(n_ao, 128)
    c_col = pick(dot(facts.astype(BF16), slot_pick), own_col)
    c_live = pick(jnp.broadcast_to(facts[:, SLOTS:SLOTS + 1], (n_ao, n_c)), own_col)
    col_big = pick(size_all, atom_col.astype(F32) == c_col) > 16.5
    alive = c_slot.astype(F32) < c_live
    one = jnp.ones((1, n_c), F32)
    nil = jnp.zeros((1, n_c), F32)
    big = jnp.where(row_big, one, nil)
    wide = jnp.where(col_big, one, nil)
    here = jnp.where(alive, one, nil)
    is4 = here * big * wide
    is2r = here * big * (one - wide)
    is2c = here * (one - big) * wide
    is1 = here * (one - big) * (one - wide)
    marks = jnp.concatenate([is4, is2c, is2r, is1, jnp.zeros((12, n_c), F32)], axis=0)
    marks = [marks[:, i * 128:(i + 1) * 128] for i in range(n_c // 128)]
    inside = dot(jnp.concatenate(marks, axis=0).astype(BF16), earlier)
    before, count = [], jnp.zeros((16, 1), F32)
    for i, block in enumerate(marks):
        before.append(inside[i * 16:(i + 1) * 16] + count)
        count = count + lane_sum(block) * 0.5
    before = jnp.concatenate(before, axis=1)
    base2c = 4.0 * count[0:1]
    base2r = base2c + 4.0 * jnp.floor((count[1:2] + 1.0) * 0.5)
    base1 = base2r + 2.0 * count[2:3]
    total = base1 + count[3:4]
    twos = jnp.floor(before[1:2] * 0.5)
    first = is4 * 4.0 * before[0:1] + is2c * (base2c + before[1:2] + 2.0 * twos)
    first = first + is2r * (base2r + 2.0 * before[2:3]) + is1 * (base1 + before[3:4])
    c_auxf = c_aux.astype(F32)

    def numbered(member, offset):
        return jnp.where(member > 0.5, 2.0 * (first + offset) + c_auxf, -5.0)

    units = [
        numbered(here, 0.0),
        numbered(is4 + is2c, 2.0),
        numbered(is4 + is2r, 1.0),
        numbered(is4, 3.0),
    ]
    flag_ref[...] = jnp.where(total > 4.0 * sum(caps) * (n_ao // CORES), 1, 0)

    unit_lanes = jnp.concatenate(units, axis=1)
    my_half = my_in // n_y
    my_lo = lax.rem(my_in, n_y)
    turns = 2 * n_x

    out_row = iota((span * n_y * 8, 1), 0)
    out_lo, out_slot = out_row // 8 % n_y, out_row // (8 * n_y)
    out_core = out_lo % CORES
    out_first = (out_lo // CORES) * sum(caps) + out_core * caps[0] + out_slot
    out_unit = out_first * 8 + (out_row % 4) * 2 + out_row // 4 % 2
    out_keep = out_slot < jnp.where(out_core == 0, caps[0], caps[1])

    def pack(turn):
        grp = lax.rem(my_x + turn // 2, n_x) * 2 + lax.rem(my_half + turn, 2)
        wanted = jnp.where(out_keep, out_unit + grp * (n_y // CORES * sum(caps) * 8), -99).astype(F32)
        got = dot(ones_where(unit_lanes == wanted), bq[...].reshape(4 * n_c, QUART))
        for j in range(span):
            part = got[j * n_y * 8:(j + 1) * n_y * 8]
            both = [part[:, h * HALF:(h + 1) * HALF].reshape(n_y, 8, HALF) for h in range(2)]
            send[pl.ds(grp * n_y, n_y), :, j * HALF:(j + 1) * HALF] = jnp.concatenate(both, axis=1).astype(BF16)

        def ship(step, inner):
            peer = grp * n_y + lax.rem(my_lo + step, n_y)

            def act(c, count):
                source = send.at[peer, :, pl.ds(0, count * HALF)]
                target = recv.at[me, :, pl.ds(0, count * HALF)]

                @pl.when(peer != me)
                def _():
                    pltpu.make_async_remote_copy(
                        src_ref=source, dst_ref=target, send_sem=send_sem.at[c], recv_sem=recv_sem.at[turn],
                        device_id=(zz, peer), device_id_type=MESH,
                    ).start()

                @pl.when(peer == me)
                def _():
                    pltpu.make_async_copy(source, target, recv_sem.at[turn]).start()

            by_core(lax.rem(peer, CORES), act)
            return inner

        lax.fori_loop(0, n_y, ship, 0)

    def origin(turn):
        return lax.rem(my_x + n_x - turn // 2, n_x) * 2 + lax.rem(my_half + turn, 2)

    def forward(turn):
        def act(c, count):
            block = (pl.ds(origin(turn) * n_y, n_y), slice(None), pl.ds(0, count * HALF))
            wait_bytes(recv.at[block], recv_sem.at[turn])
            pltpu.make_async_remote_copy(
                src_ref=recv.at[block], dst_ref=zup.at[block], send_sem=zs_sem, recv_sem=zu_sem.at[turn],
                device_id=(above, me), device_id_type=MESH,
            ).start()

        by_core(my_core, act)

    lag = 3

    def pack_and_forward(turn, carry):
        pack(turn)
        pl.when(turn >= lag)(lambda: forward(turn - lag))
        return carry

    lax.fori_loop(0, turns, pack_and_forward, 0)

    pair = iota((span * 16, 1), 0)
    slot_base = ((me // CORES) * sum(caps) + my_core * caps[0] + pair // 16) * 4
    lead = ((slot_base + pair // 4 % 4) * 2).astype(F32)
    tail = ((slot_base + pair % 4) * 2).astype(F32)
    c_tile = (c_row // 2).astype(F32)

    def describe(unit):
        tile, atom, col, quarter, valid = (jnp.zeros((span * 16, 1), F32) for _ in range(5))
        for q in range(4):
            hit = units[q] == unit
            tile = tile + lane_sum(jnp.where(hit, c_tile, 0.0))
            atom = atom + lane_sum(jnp.where(hit, c_atom.astype(F32), 0.0))
            col = col + lane_sum(jnp.where(hit, c_col, 0.0))
            count = lane_sum(jnp.where(hit, 1.0, 0.0))
            quarter = quarter + q * count
            valid = valid + count
        row_half = jnp.where(quarter > 1.5, 1.0, 0.0)
        return tile, atom, col, row_half, quarter - 2.0 * row_half, valid

    tile_a, atom_a, col_a, mh_a, nh_a, valid_a = describe(lead)
    tile_b, _, _, mh_b, nh_b, valid_b = describe(tail)
    joined = (tile_a == tile_b) & (valid_a > 0.5) & (valid_b > 0.5)
    index1 = jnp.where(joined & (nh_a == nh_b), atom_a * 16.0 + 4.0 * mh_b, -99.0)
    index2 = jnp.where(joined & (mh_a == mh_b), col_a * 16.0 + 8.0 + 4.0 * nh_a, -99.0)
    wait_bytes(table.at[pl.ds(0, n_far)], table_sem.at[1])
    greens = table[...].reshape(n_ao * 16, 128)
    g_row = iota((span * 16, n_ao * 16), 1)
    g_spot = g_row // 16
    g_atom = device(g_spot // n_y % n_x, g_spot % n_y, g_spot // (n_x * n_y))
    g_lane = (g_atom * 16 + g_row % 16).astype(F32)
    for target, index, half in ((v1, index1, mh_a), (v2, index2, nh_b)):
        rows = [dot(ones_where(g_lane == index + i), greens).astype(BF16) for i in range(4)]
        rows = dot(jnp.concatenate(rows, axis=1), mover)
        target[...] = jnp.where(half < 0.5, rows[:, :QUART], rows[:, QUART:])

    r, s = iota((QUART, QUART), 0), iota((QUART, QUART), 1)
    hi, lo = r // 16, r % 16
    spread1, gather1, keep1 = ones_where(hi == s % 16), ones_where(hi == s // 16), ones_where(lo == s % 16)
    spread2, gather2, keep2 = ones_where(lo == s // 16), ones_where(lo == s % 16), ones_where(hi == s // 16)

    def weights(j):
        for m in range(2):
            for a in range(2):
                for b in range(2):
                    rows, lanes = slice(a * QUART, (a + 1) * QUART), slice(b * QUART, (b + 1) * QUART)
                    vec = v1[pl.ds(j * 16 + (2 * m + a) * 4 + 2 * m + b, 1), :].astype(BF16)
                    w1[j, m, rows, lanes] = dot(spread1 * vec, gather1).astype(BF16) * keep1
                    vec = v2[pl.ds(j * 16 + (2 * a + m) * 4 + 2 * b + m, 1), :].astype(BF16)
                    w2[j, m, rows, lanes] = dot(spread2 * vec, gather2).astype(BF16) * keep2

    o, i = iota((n_y * 16, n_y * 16), 0), iota((n_y * 16, n_y * 16), 1)
    went = (i // 8 % 2 * 4 + i % 4) * (2 * n_y) + (i // 16) * 2 + i // 4 % 2
    sorter = ones_where(o == went)

    def unpack(source, turn, target):
        grp = origin(turn)
        block = source[pl.ds(grp * n_y, n_y)].reshape(n_y * 16, span * HALF)
        placed = dot(sorter, block).astype(BF16)
        rows = pl.ds(pl.multiple_of(grp * (2 * n_y), 2 * n_y), 2 * n_y)
        for h in range(2):
            for b in range(4):
                part = placed[(h * 4 + b) * 2 * n_y:(h * 4 + b + 1) * 2 * n_y]
                for j in range(span):
                    target[j, rows, b * QUART + h * HALF:b * QUART + (h + 1) * HALF] = part[:, j * HALF:(j + 1) * HALF]

    def contract(tiles, j):
        half = [dot(tiles[:, m * 512:(m + 1) * 512], w1[j, m]).astype(BF16) for m in range(2)]
        done = []
        for m in range(2):
            lanes = slice(m * QUART, (m + 1) * QUART)
            done.append(dot(jnp.concatenate([part[:, lanes] for part in half], axis=1), w2[j, m]).astype(BF16))
        return jnp.concatenate([done[m][:, a * QUART:(a + 1) * QUART] for a in range(2) for m in range(2)], axis=1)

    def weights_and_forward(j, carry):
        weights(j)
        for turn in range(turns - lag, turns):
            pl.when(j == (turn - turns + lag) * span // lag)(functools.partial(forward, turn))
        return carry

    lax.fori_loop(0, span, weights_and_forward, 0)

    def arrive(turn, carry):
        unpack(recv, turn, masked)
        return carry

    lax.fori_loop(0, turns, arrive, 0)

    same[...] = jnp.zeros_like(same)

    def own_slot(j, carry):
        tiles = masked[j]
        same[...] += dot_nt(contract(tiles, j), tiles)
        return carry

    lax.fori_loop(0, span, own_slot, 0)

    def reduce_x(c, part):
        for a in range(n_a):
            for e in range(2):
                start = (a // CORES) * n_grp * 2 + (a % CORES) * 2 + e
                rs_a[c, a, e * n_y:(e + 1) * n_y, :] = part[pl.ds(start, n_y, stride=4), :]
        rs_a_in[c, pl.ds(mine, 1)] = rs_a[c, pl.ds(mine, 1)]
        for step in range(1, n_a):
            to = lax.rem(mine + step, n_a)
            pltpu.make_async_remote_copy(
                src_ref=rs_a.at[c, to], dst_ref=rs_a_in.at[c, mine], send_sem=rs_sem.at[c], recv_sem=rs_sem.at[2 + c],
                device_id=(zz, device(to // CORES, my_y, lax.rem(to, CORES))), device_id_type=MESH,
            ).start()

    def reduced_x(c):
        wait_bytes(rs_a_in.at[c, pl.ds(0, n_a - 1)], rs_sem.at[2 + c])
        rs_mid[c * 2 * n_y:(c + 1) * 2 * n_y, :] = jnp.sum(rs_a_in[c], axis=0)

    reduce_x(0, same)

    def arrive_up(turn, carry):
        def act(c, count):
            wait_bytes(zup.at[pl.ds(origin(turn) * n_y, n_y), :, pl.ds(0, count * HALF)], zu_sem.at[turn])

        by_core(my_core, act)
        unpack(zup, turn, masked_up)
        return carry

    lax.fori_loop(0, turns, arrive_up, 0)
    cross[...] = jnp.zeros_like(cross)

    def up_slot(j, carry):
        cross[...] += dot_nt(contract(masked_up[j], j), masked[j])
        return carry

    lax.fori_loop(0, span, up_slot, 0)
    reduce_x(1, cross)
    reduced_x(0)
    reduced_x(1)
    for y in range(n_y):
        rs_b[y, 0:4, :] = rs_mid[pl.ds(y, 4, stride=n_y), :]
        rs_b[y, 4:8, :] = jnp.zeros((4, n_p), F32)
    rs_b_in[pl.ds(my_y, 1)] = rs_b[pl.ds(my_y, 1)]
    for step in range(1, n_y):
        to = lax.rem(my_y + step, n_y)
        pltpu.make_async_remote_copy(
            src_ref=rs_b.at[to], dst_ref=rs_b_in.at[my_y], send_sem=rs_sem.at[4], recv_sem=rs_sem.at[5],
            device_id=(zz, device(my_x, to, my_core)), device_id_type=MESH,
        ).start()
    wait_bytes(rs_b_in.at[pl.ds(0, n_y - 1)], rs_sem.at[5])
    final = jnp.sum(rs_b_in[...], axis=0)
    out_ref[0] = final[0:2]
    out_ref[1] = final[2:4]

    wait_bytes(meta.at[pl.ds(0, n_y - 1)], small_send.at[0])
    wait_bytes(table.at[pl.ds(0, n_y - 1)], small_send.at[1])
    wait_bytes(meta.at[pl.ds(0, n_far)], small_send.at[2])
    wait_bytes(table.at[pl.ds(0, n_far)], small_send.at[3])
    if caps[0] == caps[1]:
        wait_bytes(send.at[pl.ds(0, n_ao - 1)], send_sem.at[0])
    else:
        for c in range(CORES):
            lanes = pl.ds(0, caps[c] * HALF)

            @pl.when(my_core == c)
            def _():
                wait_bytes(send.at[pl.ds(0, n_ao // CORES - 1), :, lanes], send_sem.at[c])

            @pl.when(my_core != c)
            def _():
                wait_bytes(send.at[pl.ds(0, n_ao // CORES), :, lanes], send_sem.at[c])

    def sent_up(c, count):
        wait_bytes(zup.at[:, :, pl.ds(0, count * HALF)], zs_sem)

    by_core(my_core, sent_up)
    for c in range(2):
        wait_bytes(rs_a.at[c, pl.ds(0, n_a - 1)], rs_sem.at[c])
    wait_bytes(rs_b.at[pl.ds(0, n_y - 1)], rs_sem.at[4])


def run(caps, shape, ident, b_source, pair_cols, live_slots, g_occ, g_virt, atom_sizes):
    n_x, n_y, n_z = shape
    n_ao = n_x * n_y * CORES
    n_c, n_p = n_ao * SLOTS * 2, 2 * n_ao
    n_a = n_x * CORES
    span = max(caps)
    vmem = pl.BlockSpec(memory_space=pltpu.VMEM)
    dma = pltpu.SemaphoreType.DMA
    return pl.pallas_call(
        functools.partial(kernel, (caps, n_x, n_y, n_z)),
        out_shape=(jax.ShapeDtypeStruct((2, 2, n_p), F32), jax.ShapeDtypeStruct((1, 1), jnp.int32)),
        in_specs=[pl.BlockSpec(memory_space=pl.ANY)] + [vmem] * 5,
        out_specs=(vmem, vmem),
        scratch_shapes=[
            pltpu.VMEM((n_ao, SLOTS, 2, TILE), BF16),
            pltpu.VMEM((4, n_c, QUART), BF16),
            pltpu.VMEM((n_ao, 1, 128), F32),
            pltpu.VMEM((n_ao, 16, 128), BF16),
            pltpu.VMEM((n_ao, 16, span * HALF), BF16),
            pltpu.VMEM((n_ao, 16, span * HALF), BF16),
            pltpu.VMEM((n_ao, 16, span * HALF), BF16),
            pltpu.VMEM((span, n_p, TILE), BF16),
            pltpu.VMEM((span, n_p, TILE), BF16),
            pltpu.VMEM((span, 2, 512, 512), BF16),
            pltpu.VMEM((span, 2, 512, 512), BF16),
            pltpu.VMEM((span * 16, QUART), F32),
            pltpu.VMEM((span * 16, QUART), F32),
            pltpu.VMEM((n_p, n_p), F32),
            pltpu.VMEM((n_p, n_p), F32),
            pltpu.VMEM((2, n_a, 2 * n_y, n_p), F32),
            pltpu.VMEM((2, n_a, 2 * n_y, n_p), F32),
            pltpu.VMEM((4 * n_y, n_p), F32),
            pltpu.VMEM((n_y, 8, n_p), F32),
            pltpu.VMEM((n_y, 8, n_p), F32),
            dma, dma((2,)), dma((2,)), dma((4,)), dma((2,)), dma((2 * n_x,)), dma, dma((2 * n_x,)), dma((6,)),
        ],
        compiler_params=pltpu.CompilerParams(
            collective_id=ident, has_side_effects=True, vmem_limit_bytes=56 * 1024 * 1024
        ),
        name=f"blocks_{sum(caps)}",
    )(b_source, pair_cols, live_slots, g_occ, g_virt, atom_sizes)


def whole(shape, values):
    return run((8, 8), shape, 1, *values)[0]


def local(shape, b_source, g_occ, g_virt, atom_sizes, pair_cols, live_slots):
    given = (b_source, pair_cols, live_slots.reshape(1, 1), g_occ, g_virt, atom_sizes.reshape(1, -1))
    short, flag = run((4, 3), shape, 0, *given)
    return lax.cond(
        flag[0, 0] > 0, lambda *values: whole(shape, values), lambda *values: short, *given
    )


def solution(mesh):
    n_ao, n_z = mesh.shape["ao"], mesh.shape["aux"]
    n_x = 4 if n_ao >= 64 else 2
    return jax.shard_map(
        functools.partial(local, (n_x, n_ao // (n_x * CORES), n_z)),
        mesh=mesh,
        in_specs=(
            P(None, None, ("aux", "ao"), None),
            P("ao", None),
            P("ao", None),
            P(),
            P("ao", None),
            P("ao"),
        ),
        out_specs=P(None, ("aux", "ao"), None),
        check_vma=False,
    )
```

time: 413 us -> 78.9 us (0.19)
  waiting for transfers between devices: 250 us -> 0 us
  blocking collectives: 77.8 us -> 0 us
  Pallas kernels: 0 us -> 76.3 us
  local copies, waits for them, and re-layouts: 36.5 us -> 0.6 us
  starting transfers between devices: 20.7 us -> 0 us
  between operations: 14.9 us -> 1.56 us
  matrix products: 9.68 us -> 0 us
    unnamed x2 -> x0, waiting for transfers between devices: 197 us -> none
    all_gather x1 -> x0, blocking collectives: 77.8 us -> none  [local(): all_virt = lax.all_gather(g_virt, 'ao', axis=0, tiled=True)]
    pallas_call x0 -> x1, Pallas kernels: none -> 76.3 us  [run(): pl.pallas_call(functools.partial(kernel, (caps, n_x, n_y, n_z)), out_shap...]
    ppermute x1 -> x0, waiting for transfers between devices: 52.4 us -> none  [shifted(): return lax.ppermute(value, axis, pairs)]
    mul x2 -> x0, local copies, waits for them, and re-layouts: 24.2 us -> none  [local(): masked = remapped * pad_mask[:, :, None, :]]
    all_to_all x1 -> x0, starting transfers between devices: 18.4 us -> none  [local(): lax.all_to_all(b_source, 'ao', split_axis=0, concat_axis=2, tiled=True)]
    dot_general x4 -> x0, matrix products: 9.68 us -> none  [the longest x1 2.57 us: local(): jnp.einsum('rkpb,rkqb->pq', prior_terms, masked, preferred_element_type=j...]
    unnamed x14 -> x11, local copies, waits for them, and re-layouts: 6.15 us -> 0.6 us
  transfers between devices with their start and end apart: 3 -> 0, of which waited for: 2 -> 0; matrix products, arithmetic and copies ran while one was open for 2% -> 0% of each run, Pallas kernels for 0% -> 0%
where the time goes in v2:
time: 78.9 us; the launch traced here: 78.7 us
  Pallas kernels  76.3 us (97%)
  between operations  1.56 us (2%)
    pallas_call x1, Pallas kernels, run(): pl.pallas_call(functools.partial(kernel, (caps, n_x, n_y, n_z)), out_shap...  76.3 us

profile of v2, /device:TPU:1, one launch (start us, length us, event | category | flops | bytes accessed | tf_op | source)
XLA Modules:
  0.0 78.7 jit_solution(16873672082904745683)
XLA Ops:
  0.0 0.0 copy-start.3
  0.0 0.0 copy-start.2
  0.0 0.0 copy-start.1
  0.0 0.0 copy-start
  0.0 0.0 copy-start.4
  0.8 76.3 %blocks_7.1 = (f32[2,2,128]{2,1,0:T(2,128)S(1)}, s32[1,1]{1,0:T(1,128)}) custom-call(bf16[64,8,2,1024]{3,2,1,0:T(2,128)(2,1)} %b_hbm.1, s32[1,8]{1,0:T(1,128)} %pairs_own.1, s32[1,1]{1,0:T(1,128)} %bitcast.3.live_own, bf16[1,1024]{1,0:T(2,128)(2,1)} %occ_own.1, bf16[1,1024]{1,0:T(2,128)(2,1)} %virt_own.1, s32[1,64]{1,0:T(1,128)} %bitcast.4), custom_call_target="tpu_custom_call" | custom-call | tf_op jit(solution)/shard_map/blocks_7/pallas_call | solution.py:469
  77.8 0.0 copy-done.3
  77.8 0.0 copy-done.2
  77.9 0.0 copy-done.1
  77.9 0.0 copy-done
  77.9 0.0 copy-done.4
  77.9 0.2 conditional.1
  78.1 0.6 copy.13
Async XLA Ops:
  0.0 77.8 %copy-start.3 = (s32[1,8]{1,0:T(1,128)S(1)}, s32[1,8]{1,0:T(1,128)}, u32[]{:S(2)}) copy-start(s32[1,8]{1,0:T(1,128)} %pairs_own.1) | copy-start | bytes 100
  0.0 77.8 %copy-start.2 = (bf16[1,1024]{1,0:T(2,128)(2,1)S(1)}, bf16[1,1024]{1,0:T(2,128)(2,1)}, u32[]{:S(2)}) copy-start(bf16[1,1024]{1,0:T(2,128)(2,1)} %virt_own.1) | copy-start | bytes 6148
  0.0 77.9 %copy-start.1 = (bf16[1,1024]{1,0:T(2,128)(2,1)S(1)}, bf16[1,1024]{1,0:T(2,128)(2,1)}, u32[]{:S(2)}) copy-start(bf16[1,1024]{1,0:T(2,128)(2,1)} %occ_own.1) | copy-start | bytes 6148
  0.0 77.9 %copy-start = (bf16[64,8,2,1024]{3,2,1,0:T(2,128)(2,1)S(1)}, bf16[64,8,2,1024]{3,2,1,0:T(2,128)(2,1)}, u32[]{:S(2)}) copy-start(bf16[64,8,2,1024]{3,2,1,0:T(2,128)(2,1)} %b_hbm.1) | copy-start | bytes 6291460
  0.0 77.9 %copy-start.4 = (s32[64]{0:T(128)S(1)}, s32[64]{0:T(128)}, u32[]{:S(2)}) copy-start(s32[64]{0:T(128)} %param.11) | copy-start | bytes 772

commit v3 on v2

--- a/solution.py
+++ b/solution.py
@@ -49,7 +49,7 @@
 def kernel(
     dims, b_hbm, pairs_own, live_own, occ_own, virt_own, sizes, out_ref, flag_ref,
     b_in, bq, meta, table, send, recv, zup, masked, masked_up, w1, w2, v1, v2,
-    same, cross, rs_a, rs_a_in, rs_mid, rs_b, rs_b_in,
+    same, cross, rs, rs_in,
     b_sem, meta_sem, table_sem, small_send, send_sem, recv_sem, zs_sem, zu_sem, rs_sem,
 ):
     caps, n_x, n_y, n_z = dims
@@ -103,7 +103,7 @@
         return carry
 
     pl.semaphore_signal(barrier, inc=1, device_id=(below, me), device_id_type=MESH)
-    lax.fori_loop(1, n_ao, greet, 0)
+    lax.fori_loop(1, n_ao, greet, 0, unroll=7)
 
     lane_in, lane_out = iota((512, 512), 0), iota((512, 512), 1)
     moved = (lane_in // 16 % 2) * 256 + (lane_in // 32) * 16 + lane_in % 16
@@ -150,13 +150,19 @@
         lax.fori_loop(1, n_a, one, 0)
 
     n_far = (n_a - 1) * n_y
-    spread_y(meta, small_send.at[0], meta_sem.at[0])
+
+    def tell(step, carry):
+        peer = lax.rem(me + step, n_ao)
+        pltpu.make_async_remote_copy(
+            src_ref=meta.at[spot], dst_ref=meta.at[spot], send_sem=small_send.at[0], recv_sem=meta_sem,
+            device_id=(zz, peer), device_id_type=MESH,
+        ).start()
+        return carry
+
+    lax.fori_loop(1, n_ao, tell, 0, unroll=7)
+    spread_y(table, small_send.at[1], table_sem.at[0])
     load_b.wait()
-    lax.fori_loop(0, 2, reorder, 0)
-    wait_bytes(meta.at[pl.ds(0, n_y - 1)], meta_sem.at[0])
-    spread_x(meta, small_send.at[2], meta_sem.at[1])
-    spread_y(table, small_send.at[1], table_sem.at[0])
-    lax.fori_loop(2, 4, reorder, 0)
+    lax.fori_loop(0, 4, reorder, 0)
 
     c_row = iota((1, n_c), 1)
     c_atom, c_slot, c_aux = c_row // 16, c_row // 2 % 8, c_row % 2
@@ -171,8 +177,8 @@
     row_big = pick(size_all, atom_col == iota((n_ao, n_c), 1) // 16) > 16.5
 
     wait_bytes(table.at[pl.ds(0, n_y - 1)], table_sem.at[0])
-    spread_x(table, small_send.at[3], table_sem.at[1])
-    wait_bytes(meta.at[pl.ds(0, n_far)], meta_sem.at[1])
+    spread_x(table, small_send.at[2], table_sem.at[1])
+    wait_bytes(meta.at[pl.ds(0, n_ao - 1)], meta_sem)
     facts = meta[...].reshape(n_ao, 128)
     c_col = pick(dot(facts.astype(BF16), slot_pick), own_col)
     c_live = pick(jnp.broadcast_to(facts[:, SLOTS:SLOTS + 1], (n_ao, n_c)), own_col)
@@ -216,9 +222,18 @@
     flag_ref[...] = jnp.where(total > 4.0 * sum(caps) * (n_ao // CORES), 1, 0)
 
     unit_lanes = jnp.concatenate(units, axis=1)
-    my_half = my_in // n_y
-    my_lo = lax.rem(my_in, n_y)
+    n_half = n_y // 2
+    my_odd = lax.rem(my_y, 2)
     turns = 2 * n_x
+
+    def place(x, y, core):
+        return ((x * 2 + lax.rem(y, 2)) * n_half + y // 2) * CORES + core
+
+    my_place = place(my_x, my_y, my_core)
+
+    def offset(even, k):
+        odd_off, even_off = (1, -1, 3, -3)[k], (2, -2, 4, 0)[k]
+        return odd_off + even * (even_off - odd_off)
 
     out_row = iota((span * n_y * 8, 1), 0)
     out_lo, out_slot = out_row // 8 % n_y, out_row // (8 * n_y)
@@ -228,7 +243,9 @@
     out_keep = out_slot < jnp.where(out_core == 0, caps[0], caps[1])
 
     def pack(turn):
-        grp = lax.rem(my_x + turn // 2, n_x) * 2 + lax.rem(my_half + turn, 2)
+        to_x = lax.rem(my_x + turn // 2, n_x)
+        even = lax.rem(turn, 2)
+        grp = to_x * 2 + lax.rem(my_odd + 1 + even, 2)
         wanted = jnp.where(out_keep, out_unit + grp * (n_y // CORES * sum(caps) * 8), -99).astype(F32)
         got = dot(ones_where(unit_lanes == wanted), bq[...].reshape(4 * n_c, QUART))
         for j in range(span):
@@ -236,42 +253,48 @@
             both = [part[:, h * HALF:(h + 1) * HALF].reshape(n_y, 8, HALF) for h in range(2)]
             send[pl.ds(grp * n_y, n_y), :, j * HALF:(j + 1) * HALF] = jnp.concatenate(both, axis=1).astype(BF16)
 
-        def ship(step, inner):
-            peer = grp * n_y + lax.rem(my_lo + step, n_y)
+        for k in range(n_half):
+            to_y = lax.rem(my_y + n_y + offset(even, k), n_y)
+            for flip in range(CORES):
+                core = lax.rem(my_core + flip, CORES)
+                peer = device(to_x, to_y, core)
+                at = place(to_x, to_y, core)
+
+                def act(c, count):
+                    source = send.at[at, :, pl.ds(0, count * HALF)]
+                    target = recv.at[my_place, :, pl.ds(0, count * HALF)]
+
+                    @pl.when(peer != me)
+                    def _():
+                        pltpu.make_async_remote_copy(
+                            src_ref=source, dst_ref=target, send_sem=send_sem.at[c], recv_sem=recv_sem.at[turn * n_half + k],
+                            device_id=(zz, peer), device_id_type=MESH,
+                        ).start()
+
+                    @pl.when(peer == me)
+                    def _():
+                        pltpu.make_async_copy(source, target, recv_sem.at[turn * n_half + k]).start()
+
+                by_core(core, act)
+
+    def origin(turn):
+        return lax.rem(my_x + n_x - turn // 2, n_x) * 2 + lax.rem(my_odd + 1 + turn, 2)
+
+    def forward(turn):
+        from_x = lax.rem(my_x + n_x - turn // 2, n_x)
+        for k in range(n_half):
+            from_y = lax.rem(my_y + n_y - offset(lax.rem(turn, 2), k), n_y)
+            chip = place(from_x, from_y, 0)
 
             def act(c, count):
-                source = send.at[peer, :, pl.ds(0, count * HALF)]
-                target = recv.at[me, :, pl.ds(0, count * HALF)]
-
-                @pl.when(peer != me)
-                def _():
-                    pltpu.make_async_remote_copy(
-                        src_ref=source, dst_ref=target, send_sem=send_sem.at[c], recv_sem=recv_sem.at[turn],
-                        device_id=(zz, peer), device_id_type=MESH,
-                    ).start()
-
-                @pl.when(peer == me)
-                def _():
-                    pltpu.make_async_copy(source, target, recv_sem.at[turn]).start()
-
-            by_core(lax.rem(peer, CORES), act)
-            return inner
-
-        lax.fori_loop(0, n_y, ship, 0)
-
-    def origin(turn):
-        return lax.rem(my_x + n_x - turn // 2, n_x) * 2 + lax.rem(my_half + turn, 2)
-
-    def forward(turn):
-        def act(c, count):
-            block = (pl.ds(origin(turn) * n_y, n_y), slice(None), pl.ds(0, count * HALF))
-            wait_bytes(recv.at[block], recv_sem.at[turn])
-            pltpu.make_async_remote_copy(
-                src_ref=recv.at[block], dst_ref=zup.at[block], send_sem=zs_sem, recv_sem=zu_sem.at[turn],
-                device_id=(above, me), device_id_type=MESH,
-            ).start()
-
-        by_core(my_core, act)
+                block = (pl.ds(chip, CORES), slice(None), pl.ds(0, count * HALF))
+                wait_bytes(recv.at[block], recv_sem.at[turn * n_half + k])
+                pltpu.make_async_remote_copy(
+                    src_ref=recv.at[block], dst_ref=zup.at[block], send_sem=zs_sem, recv_sem=zu_sem.at[turn],
+                    device_id=(above, me), device_id_type=MESH,
+                ).start()
+
+            by_core(my_core, act)
 
     lag = 3
 
@@ -283,7 +306,7 @@
     lax.fori_loop(0, turns, pack_and_forward, 0)
 
     pair = iota((span * 16, 1), 0)
-    slot_base = ((me // CORES) * sum(caps) + my_core * caps[0] + pair // 16) * 4
+    slot_base = ((my_place // CORES) * sum(caps) + my_core * caps[0] + pair // 16) * 4
     lead = ((slot_base + pair // 4 % 4) * 2).astype(F32)
     tail = ((slot_base + pair % 4) * 2).astype(F32)
     c_tile = (c_row // 2).astype(F32)
@@ -371,31 +394,39 @@
 
     same[...] = jnp.zeros_like(same)
 
+    q, p = iota((n_p, n_p), 0), iota((n_p, n_p), 1)
+    straight = ones_where(place(q // (4 * n_y), q // 4 % n_y, q // 2 % 2) * 2 + q % 2 == p)
+
     def own_slot(j, carry):
         tiles = masked[j]
-        same[...] += dot_nt(contract(tiles, j), tiles)
+        ordered = dot(straight, tiles).astype(BF16)
+        same[...] += dot_nt(contract(tiles, j), ordered)
+        masked[j] = ordered
         return carry
 
     lax.fori_loop(0, span, own_slot, 0)
 
-    def reduce_x(c, part):
-        for a in range(n_a):
-            for e in range(2):
-                start = (a // CORES) * n_grp * 2 + (a % CORES) * 2 + e
-                rs_a[c, a, e * n_y:(e + 1) * n_y, :] = part[pl.ds(start, n_y, stride=4), :]
-        rs_a_in[c, pl.ds(mine, 1)] = rs_a[c, pl.ds(mine, 1)]
-        for step in range(1, n_a):
-            to = lax.rem(mine + step, n_a)
+    def scatter(c, part):
+        for e in range(2):
+            rs[c, :, e, :] = part[pl.ds(e, n_ao, stride=2), :]
+        rs_in[c, pl.ds(my_place, 1)] = rs[c, pl.ds(my_place, 1)]
+
+        def one(step, carry):
+            peer = lax.rem(me + step, n_ao)
+            at = place(peer // n_grp, peer // CORES % n_y, peer % CORES)
             pltpu.make_async_remote_copy(
-                src_ref=rs_a.at[c, to], dst_ref=rs_a_in.at[c, mine], send_sem=rs_sem.at[c], recv_sem=rs_sem.at[2 + c],
-                device_id=(zz, device(to // CORES, my_y, lax.rem(to, CORES))), device_id_type=MESH,
+                src_ref=rs.at[c, at], dst_ref=rs_in.at[c, my_place], send_sem=rs_sem.at[c], recv_sem=rs_sem.at[2 + c],
+                device_id=(zz, peer), device_id_type=MESH,
             ).start()
-
-    def reduced_x(c):
-        wait_bytes(rs_a_in.at[c, pl.ds(0, n_a - 1)], rs_sem.at[2 + c])
-        rs_mid[c * 2 * n_y:(c + 1) * 2 * n_y, :] = jnp.sum(rs_a_in[c], axis=0)
-
-    reduce_x(0, same)
+            return carry
+
+        lax.fori_loop(1, n_ao, one, 0, unroll=7)
+
+    def gather(c):
+        wait_bytes(rs_in.at[c, pl.ds(0, n_ao - 1)], rs_sem.at[2 + c])
+        out_ref[c] = jnp.sum(rs_in[c], axis=0)
+
+    scatter(0, same)
 
     def arrive_up(turn, carry):
         def act(c, count):
@@ -413,28 +444,13 @@
         return carry
 
     lax.fori_loop(0, span, up_slot, 0)
-    reduce_x(1, cross)
-    reduced_x(0)
-    reduced_x(1)
-    for y in range(n_y):
-        rs_b[y, 0:4, :] = rs_mid[pl.ds(y, 4, stride=n_y), :]
-        rs_b[y, 4:8, :] = jnp.zeros((4, n_p), F32)
-    rs_b_in[pl.ds(my_y, 1)] = rs_b[pl.ds(my_y, 1)]
-    for step in range(1, n_y):
-        to = lax.rem(my_y + step, n_y)
-        pltpu.make_async_remote_copy(
-            src_ref=rs_b.at[to], dst_ref=rs_b_in.at[my_y], send_sem=rs_sem.at[4], recv_sem=rs_sem.at[5],
-            device_id=(zz, device(my_x, to, my_core)), device_id_type=MESH,
-        ).start()
-    wait_bytes(rs_b_in.at[pl.ds(0, n_y - 1)], rs_sem.at[5])
-    final = jnp.sum(rs_b_in[...], axis=0)
-    out_ref[0] = final[0:2]
-    out_ref[1] = final[2:4]
-
-    wait_bytes(meta.at[pl.ds(0, n_y - 1)], small_send.at[0])
+    scatter(1, cross)
+    gather(0)
+    gather(1)
+
+    wait_bytes(meta.at[pl.ds(0, n_ao - 1)], small_send.at[0])
     wait_bytes(table.at[pl.ds(0, n_y - 1)], small_send.at[1])
-    wait_bytes(meta.at[pl.ds(0, n_far)], small_send.at[2])
-    wait_bytes(table.at[pl.ds(0, n_far)], small_send.at[3])
+    wait_bytes(table.at[pl.ds(0, n_far)], small_send.at[2])
     if caps[0] == caps[1]:
         wait_bytes(send.at[pl.ds(0, n_ao - 1)], send_sem.at[0])
     else:
@@ -454,15 +470,13 @@
 
     by_core(my_core, sent_up)
     for c in range(2):
-        wait_bytes(rs_a.at[c, pl.ds(0, n_a - 1)], rs_sem.at[c])
-    wait_bytes(rs_b.at[pl.ds(0, n_y - 1)], rs_sem.at[4])
+        wait_bytes(rs.at[c, pl.ds(0, n_ao - 1)], rs_sem.at[c])
 
 
 def run(caps, shape, ident, b_source, pair_cols, live_slots, g_occ, g_virt, atom_sizes):
     n_x, n_y, n_z = shape
     n_ao = n_x * n_y * CORES
     n_c, n_p = n_ao * SLOTS * 2, 2 * n_ao
-    n_a = n_x * CORES
     span = max(caps)
     vmem = pl.BlockSpec(memory_space=pltpu.VMEM)
     dma = pltpu.SemaphoreType.DMA
@@ -487,12 +501,9 @@
             pltpu.VMEM((span * 16, QUART), F32),
             pltpu.VMEM((n_p, n_p), F32),
             pltpu.VMEM((n_p, n_p), F32),
-            pltpu.VMEM((2, n_a, 2 * n_y, n_p), F32),
-            pltpu.VMEM((2, n_a, 2 * n_y, n_p), F32),
-            pltpu.VMEM((4 * n_y, n_p), F32),
-            pltpu.VMEM((n_y, 8, n_p), F32),
-            pltpu.VMEM((n_y, 8, n_p), F32),
-            dma, dma((2,)), dma((2,)), dma((4,)), dma((2,)), dma((2 * n_x,)), dma, dma((2 * n_x,)), dma((6,)),
+            pltpu.VMEM((2, n_ao, 2, n_p), F32),
+            pltpu.VMEM((2, n_ao, 2, n_p), F32),
+            dma, dma, dma((2,)), dma((3,)), dma((2,)), dma((n_x * n_y,)), dma, dma((2 * n_x,)), dma((4,)),
         ],
         compiler_params=pltpu.CompilerParams(
             collective_id=ident, has_side_effects=True, vmem_limit_bytes=56 * 1024 * 1024

time: 78.9 us -> 73.8 us (0.935)
  Pallas kernels: 76.3 us -> 71.3 us
    pallas_call x1, Pallas kernels: 76.3 us -> 71.3 us  [run(): pl.pallas_call(functools.partial(kernel, (caps, n_x, n_y, n_z)), out_shap...]
where the time goes in v3:
time: 73.8 us; the launch traced here: 73.6 us
  Pallas kernels  71.3 us (97%)
  between operations  1.56 us (2%)
    pallas_call x1, Pallas kernels, run(): pl.pallas_call(functools.partial(kernel, (caps, n_x, n_y, n_z)), out_shap...  71.3 us

profile of v3, /device:TPU:1, one launch (start us, length us, event | category | flops | bytes accessed | tf_op | source)
XLA Modules:
  0.0 73.6 jit_solution(9883204678948949178)
XLA Ops:
  0.0 0.0 copy-start.3
  0.0 0.0 copy-start.2
  0.0 0.0 copy-start.1
  0.0 0.0 copy-start
  0.0 0.0 copy-start.4
  0.8 71.3 %blocks_7.1 = (f32[2,2,128]{2,1,0:T(2,128)S(1)}, s32[1,1]{1,0:T(1,128)}) custom-call(bf16[64,8,2,1024]{3,2,1,0:T(2,128)(2,1)} %b_hbm.1, s32[1,8]{1,0:T(1,128)} %pairs_own.1, s32[1,1]{1,0:T(1,128)} %bitcast.3.live_own, bf16[1,1024]{1,0:T(2,128)(2,1)} %occ_own.1, bf16[1,1024]{1,0:T(2,128)(2,1)} %virt_own.1, s32[1,64]{1,0:T(1,128)} %bitcast.4), custom_call_target="tpu_custom_call" | custom-call | tf_op jit(solution)/shard_map/blocks_7/pallas_call | solution.py:483
  72.8 0.0 copy-done.3
  72.8 0.0 copy-done.2
  72.8 0.0 copy-done.1
  72.8 0.0 copy-done
  72.9 0.0 copy-done.4
  72.9 0.2 conditional.1
  73.1 0.6 copy.13
Async XLA Ops:
  0.0 72.8 %copy-start.3 = (s32[1,8]{1,0:T(1,128)S(1)}, s32[1,8]{1,0:T(1,128)}, u32[]{:S(2)}) copy-start(s32[1,8]{1,0:T(1,128)} %pairs_own.1) | copy-start | bytes 100
  0.0 72.8 %copy-start.2 = (bf16[1,1024]{1,0:T(2,128)(2,1)S(1)}, bf16[1,1024]{1,0:T(2,128)(2,1)}, u32[]{:S(2)}) copy-start(bf16[1,1024]{1,0:T(2,128)(2,1)} %virt_own.1) | copy-start | bytes 6148
  0.0 72.8 %copy-start.1 = (bf16[1,1024]{1,0:T(2,128)(2,1)S(1)}, bf16[1,1024]{1,0:T(2,128)(2,1)}, u32[]{:S(2)}) copy-start(bf16[1,1024]{1,0:T(2,128)(2,1)} %occ_own.1) | copy-start | bytes 6148
  0.0 72.8 %copy-start = (bf16[64,8,2,1024]{3,2,1,0:T(2,128)(2,1)S(1)}, bf16[64,8,2,1024]{3,2,1,0:T(2,128)(2,1)}, u32[]{:S(2)}) copy-start(bf16[64,8,2,1024]{3,2,1,0:T(2,128)(2,1)} %b_hbm.1) | copy-start | bytes 6291460
  0.0 72.8 %copy-start.4 = (s32[64]{0:T(128)S(1)}, s32[64]{0:T(128)}, u32[]{:S(2)}) copy-start(s32[64]{0:T(128)} %param.11) | copy-start | bytes 772

commit v4 on v3

--- a/solution.py
+++ b/solution.py
@@ -120,6 +120,8 @@
             bq[2 * mh + 1, rows, :] = placed[:, QUART:]
         return carry
 
+    load_b.wait()
+    lax.fori_loop(0, 3, reorder, 0)
     pl.semaphore_wait(barrier, n_ao)
 
     def spread_y(ref, send_to, recv_from):
@@ -160,9 +162,8 @@
         return carry
 
     lax.fori_loop(1, n_ao, tell, 0, unroll=7)
+    lax.fori_loop(3, 4, reorder, 0)
     spread_y(table, small_send.at[1], table_sem.at[0])
-    load_b.wait()
-    lax.fori_loop(0, 4, reorder, 0)
 
     c_row = iota((1, n_c), 1)
     c_atom, c_slot, c_aux = c_row // 16, c_row // 2 % 8, c_row % 2

time: 73.8 us -> 73.8 us (level)
  no operation moved by 1% of the time
where the time goes in v4:
time: 73.8 us; the launch traced here: 73.6 us
  Pallas kernels  71.3 us (97%)
  between operations  1.56 us (2%)
    pallas_call x1, Pallas kernels, run(): pl.pallas_call(functools.partial(kernel, (caps, n_x, n_y, n_z)), out_shap...  71.3 us

profile of v4, /device:TPU:1, one launch (start us, length us, event | category | flops | bytes accessed | tf_op | source)
XLA Modules:
  0.0 73.6 jit_solution(559482798036279037)
XLA Ops:
  0.0 0.0 copy-start.3
  0.0 0.0 copy-start.2
  0.0 0.0 copy-start.1
  0.0 0.0 copy-start
  0.0 0.0 copy-start.4
  0.8 71.3 %blocks_7.1 = (f32[2,2,128]{2,1,0:T(2,128)S(1)}, s32[1,1]{1,0:T(1,128)}) custom-call(bf16[64,8,2,1024]{3,2,1,0:T(2,128)(2,1)} %b_hbm.1, s32[1,8]{1,0:T(1,128)} %pairs_own.1, s32[1,1]{1,0:T(1,128)} %bitcast.3.live_own, bf16[1,1024]{1,0:T(2,128)(2,1)} %occ_own.1, bf16[1,1024]{1,0:T(2,128)(2,1)} %virt_own.1, s32[1,64]{1,0:T(1,128)} %bitcast.4), custom_call_target="tpu_custom_call" | custom-call | tf_op jit(solution)/shard_map/blocks_7/pallas_call | solution.py:484
  72.8 0.0 copy-done.3
  72.8 0.0 copy-done.2
  72.8 0.0 copy-done.1
  72.8 0.0 copy-done
  72.8 0.0 copy-done.4
  72.8 0.2 conditional.1
  73.0 0.6 copy.13
Async XLA Ops:
  0.0 72.8 %copy-start.3 = (s32[1,8]{1,0:T(1,128)S(1)}, s32[1,8]{1,0:T(1,128)}, u32[]{:S(2)}) copy-start(s32[1,8]{1,0:T(1,128)} %pairs_own.1) | copy-start | bytes 100
  0.0 72.8 %copy-start.2 = (bf16[1,1024]{1,0:T(2,128)(2,1)S(1)}, bf16[1,1024]{1,0:T(2,128)(2,1)}, u32[]{:S(2)}) copy-start(bf16[1,1024]{1,0:T(2,128)(2,1)} %virt_own.1) | copy-start | bytes 6148
  0.0 72.8 %copy-start.1 = (bf16[1,1024]{1,0:T(2,128)(2,1)S(1)}, bf16[1,1024]{1,0:T(2,128)(2,1)}, u32[]{:S(2)}) copy-start(bf16[1,1024]{1,0:T(2,128)(2,1)} %occ_own.1) | copy-start | bytes 6148
  0.0 72.8 %copy-start = (bf16[64,8,2,1024]{3,2,1,0:T(2,128)(2,1)S(1)}, bf16[64,8,2,1024]{3,2,1,0:T(2,128)(2,1)}, u32[]{:S(2)}) copy-start(bf16[64,8,2,1024]{3,2,1,0:T(2,128)(2,1)} %b_hbm.1) | copy-start | bytes 6291460
  0.0 72.8 %copy-start.4 = (s32[64]{0:T(128)S(1)}, s32[64]{0:T(128)}, u32[]{:S(2)}) copy-start(s32[64]{0:T(128)} %param.11) | copy-start | bytes 772
